TPU v7x, 32 devices: a whole 2x2x4 slice. The times are simulated.
32 devices in a mesh: tok: 8 (over z, y), hid: 4 (over x, core).
Axes of the slice: x: 2, y: 2, z: 4, core: 2. Of those that a mesh axis runs over, the one named last changes fastest.
Arguments:
- queries: bfloat16 [2048, 5120], P('tok', 'hid'), may hold values from -40 to 40
- keys: bfloat16 [2048, 5120], P('tok', 'hid'), may hold values from -40 to 40
- values: bfloat16 [2048, 5120], P('tok', 'hid'), may hold values from -6 to 6
- residual: bfloat16 [2048, 5120], P('tok', 'hid'), may hold values from -62 to 62
- out_weight: bfloat16 [5120, 5120], P(None, 'hid'), may hold values from -0.078125 to 0.078125
- adapter_a: bfloat16 [64, 5120, 16], P('tok', 'hid'), may hold values from -0.078125 to 0.078125
- adapter_b: bfloat16 [64, 16, 5120], P('tok', None, 'hid'), may hold values from -1.5 to 1.5
- request_lengths: int32 [4], replicated, may hold values from 256 to 768, as said below
- request_adapter: int32 [4], replicated, may hold values from 0 to 63
- adapter_slot: int32 [64], replicated, may hold values from 0 to 63, each once
- mod_scale: float32 [5120], P('hid'), may hold values from -3 to 3
- mod_shift: float32 [5120], P('hid'), may hold values from -3 to 3
Outputs:
- stream: bfloat16 [2048, 5120], P('tok', 'hid')
- normed: bfloat16 [2048, 5120], P('tok', 'hid')
Inputs may be any that keep to these rules, and one draw needn't show every extreme that they name: `request_lengths`: each request holds 256 to 768 tokens, together all 2048; some request holds exactly 768. `adapter_slot`: each slot once.
All inputs are finite; a program needn't handle non-finite values.
Results may differ from a plain program's by a relative error of at most 0.0027.
Values may be sent and summed in bfloat16 or wider, within the bound.
A program may use at most 128 MiB of HBM per device.

v0:
```python
import math

import jax
import jax.numpy as jnp
from jax import lax
from jax.sharding import PartitionSpec as P

HEAD_DIM = 128
D = 5120
ADAPTERS = 64
REACH = 3


def shifted(value, axis, steps):
    count = lax.axis_size(axis)
    initial, last = (max(0, -steps), min(count, count - steps))
    return lax.ppermute(value, axis, [(source, source + steps) for source in range(initial, last)])


def segments_of(positions, request_lengths):
    ends = jnp.cumsum(request_lengths)
    return jnp.sum((ends[None, :] <= positions[:, None]).astype(jnp.int32), axis=1)


def on_device(
    queries,
    keys,
    values,
    residual,
    out_weight,
    adapter_a,
    adapter_b,
    request_lengths,
    request_adapter,
    adapter_slot,
    mod_scale,
    mod_shift,
):
    rows = queries.shape[0]
    local = queries.shape[1]
    heads_here = local // HEAD_DIM
    total_rows = rows * lax.axis_size("tok")
    here = lax.axis_index("tok")
    offsets = jnp.arange(rows, dtype=jnp.int32)
    own_pos = here * rows + offsets
    key_list = [keys]
    val_list = [values]
    pos_list = [own_pos]
    for offset in list(range(1, REACH + 1)) + list(range(-REACH, 0)):
        moved = shifted((keys, values), "tok", offset)
        key_list.append(moved[0])
        val_list.append(moved[1])
        pos_list.append((here - offset) * rows + offsets)
    key_all = jnp.concatenate(key_list, axis=0)
    val_all = jnp.concatenate(val_list, axis=0)
    key_pos = jnp.concatenate(pos_list, axis=0)
    key_seg = segments_of(key_pos, request_lengths)
    inside = (key_pos >= 0) & (key_pos < total_rows)
    query_seg = segments_of(own_pos, request_lengths)
    query_three = queries.reshape(rows, heads_here, HEAD_DIM)
    key_three = key_all.reshape(-1, heads_here, HEAD_DIM)
    val_three = val_all.reshape(-1, heads_here, HEAD_DIM)
    scores = jnp.einsum(
        "qhd,khd->hqk", query_three, key_three, preferred_element_type=jnp.float32
    ) / math.sqrt(HEAD_DIM)
    admit = ((query_seg[:, None] == key_seg[None, :]) & inside[None, :])[None, :, :]
    scores = jnp.where(admit, scores, -1e30)
    top = jnp.max(scores, axis=-1, keepdims=True)
    expo = jnp.exp(scores - top)
    weights = (expo / jnp.sum(expo, axis=-1, keepdims=True)).astype(jnp.bfloat16)
    attended = jnp.einsum("hqk,khd->qhd", weights, val_three, preferred_element_type=jnp.float32)
    attended = attended.astype(jnp.bfloat16).reshape(rows, local)
    projected = jnp.dot(
        lax.all_gather(attended, "hid", axis=1, tiled=True),
        out_weight,
        preferred_element_type=jnp.float32,
    )
    adapter_ids = jnp.arange(ADAPTERS, dtype=jnp.int32)
    slot_of_request = jnp.sum(
        jnp.where(request_adapter[:, None] == adapter_ids[None, :], adapter_slot[None, :], 0),
        axis=1,
    )
    request_ids = jnp.arange(request_lengths.shape[0], dtype=jnp.int32)
    bank_down, bank_up = (
        lax.all_gather(adapter_a, "tok", axis=0, tiled=True),
        lax.all_gather(adapter_b, "tok", axis=0, tiled=True),
    )
    slot_rows = jnp.sum(
        jnp.where(query_seg[:, None] == request_ids[None, :], slot_of_request[None, :], 0), axis=1
    )
    onehot = (slot_rows[:, None] == adapter_ids[None, :]).astype(jnp.float32)
    wide = jnp.einsum("rd,adk->rak", attended, bank_down, preferred_element_type=jnp.float32)
    partial_down = jnp.sum(onehot[:, :, None] * wide, axis=1)
    down = lax.psum(partial_down, "hid").astype(jnp.bfloat16)
    expand = onehot.astype(jnp.bfloat16)[:, :, None] * down[:, None, :]
    lift = jnp.einsum("rak,akd->rd", expand, bank_up, preferred_element_type=jnp.float32)
    total = residual.astype(jnp.float32) + projected + lift
    stream = total.astype(jnp.bfloat16)
    mean = lax.psum(jnp.sum(total, axis=-1), "hid")[:, None] / D
    centered = total - mean
    variance = lax.psum(jnp.sum(centered * centered, axis=-1), "hid")[:, None] / D
    normed = (centered / jnp.sqrt(variance + 1e-06) * (1.0 + mod_scale) + mod_shift).astype(
        jnp.bfloat16
    )
    return (stream, normed)


def solution(mesh):
    placed = (
        P("tok", "hid"),
        P("tok", "hid"),
        P("tok", "hid"),
        P("tok", "hid"),
        P(None, "hid"),
        P("tok", "hid", None),
        P("tok", None, "hid"),
        P(),
        P(),
        P(),
        P("hid"),
        P("hid"),
    )
    return jax.shard_map(
        on_device,
        mesh=mesh,
        in_specs=placed,
        out_specs=(P("tok", "hid"), P("tok", "hid")),
        check_vma=False,
    )
```

profile of v0, /device:TPU:0, one launch (start us, length us, event | category | flops | bytes accessed | tf_op | source)
XLA Modules:
  0.0 312.7 jit_solution(13663002790368245016)
XLA Ops:
  9.3 5.7 %collective-permute-start.6 = (bf16[256,1280]{0,1:T(8,128)(2,1)S(1)}, bf16[256,1280]{0,1:T(8,128)(2,1)}, u32[]{:S(2)}, u32[]{:S(2)}) collective-permute-start(bf16[256,1280]{0,1:T(8,128)(2,1)S(1)} %copy.55), channel_id=1, source_target_pairs={{0,4},{4,8},{8,12},{12,16},{16,20},{20,24},{24,28},{1,5},{5,9},{9,... | collective-permute-start | bytes 1966088 | tf_op jit(solution)/shard_map/ppermute | solution.py:17
  15.0 2.7 collective-permute-start.7
  17.7 4.4 %collective-permute-start.8 = (bf16[256,1280]{0,1:T(8,128)(2,1)S(1)}, bf16[256,1280]{0,1:T(8,128)(2,1)S(1)}, u32[]{:S(2)}, u32[]{:S(2)}) collective-permute-start(bf16[256,1280]{0,1:T(8,128)(2,1)S(1)} %copy.55), channel_id=1, source_target_pairs={{0,12},{4,16},{8,20},{12,24},{16,28},{1,13},{5,17},{9,21},{13,25},... | collective-permute-start | bytes 1966088 | tf_op jit(solution)/shard_map/ppermute | solution.py:17
  23.4 4.3 %collective-permute-start = (bf16[256,1280]{1,0:T(8,128)(2,1)}, bf16[256,1280]{1,0:T(8,128)(2,1)}, u32[]{:S(2)}, u32[]{:S(2)}) collective-permute-start(bf16[256,1280]{1,0:T(8,128)(2,1)} %param.14), channel_id=1, source_target_pairs={{0,4},{4,8},{8,12},{12,16},{16,20},{20,24},{24,28},{1,5},{5,9},{9,... | collective-permute-start | bytes 1966088 | tf_op jit(solution)/shard_map/ppermute | solution.py:17
  30.8 2.2 compare_and_fusion
  32.9 2.2 copy.56
  36.0 27.8 %collective-permute-start.1 = (bf16[256,1280]{1,0:T(8,128)(2,1)S(1)}, bf16[256,1280]{1,0:T(8,128)(2,1)S(1)}, u32[]{:S(2)}, u32[]{:S(2)}) collective-permute-start(bf16[256,1280]{1,0:T(8,128)(2,1)S(1)} %copy-done.1), channel_id=1, source_target_pairs={{0,8},{4,12},{8,16},{12,20},{16,24},{20,28},{1,9},{5,13},{9,17},{1... | collective-permute-start | bytes 1966088 | tf_op jit(solution)/shard_map/ppermute | solution.py:17
  65.0 5.2 %collective-permute-start.2 = (bf16[256,1280]{1,0:T(8,128)(2,1)S(1)}, bf16[256,1280]{1,0:T(8,128)(2,1)S(1)}, u32[]{:S(2)}, u32[]{:S(2)}) collective-permute-start(bf16[256,1280]{1,0:T(8,128)(2,1)S(1)} %copy-done.1), channel_id=1, source_target_pairs={{0,12},{4,16},{8,20},{12,24},{16,28},{1,13},{5,17},{9,21},{13,25},... | collective-permute-start | bytes 1966088 | tf_op jit(solution)/shard_map/ppermute | solution.py:17
  70.3 2.1 copy-done.3
  75.7 17.3 %collective-permute-done.1 = bf16[256,1280]{1,0:T(8,128)(2,1)S(1)} collective-permute-done((bf16[256,1280]{1,0:T(8,128)(2,1)S(1)}, bf16[256,1280]{1,0:T(8,128)(2,1)S(1)}, u32[]{:S(2)}, u32[]{:S(2)}) %collective-permute-start.1) | collective-permute-done | bytes 655392 | tf_op jit(solution)/shard_map/ppermute | solution.py:17
  95.1 13.7 %collective-permute-done.2 = bf16[256,1280]{1,0:T(8,128)(2,1)S(1)} collective-permute-done((bf16[256,1280]{1,0:T(8,128)(2,1)S(1)}, bf16[256,1280]{1,0:T(8,128)(2,1)S(1)}, u32[]{:S(2)}, u32[]{:S(2)}) %collective-permute-start.2) | collective-permute-done | bytes 655392 | tf_op jit(solution)/shard_map/ppermute | solution.py:17
  111.0 33.9 %collective-permute-done.3 = bf16[256,1280]{1,0:T(8,128)(2,1)S(1)} collective-permute-done((bf16[256,1280]{1,0:T(8,128)(2,1)S(1)}, bf16[256,1280]{1,0:T(8,128)(2,1)S(1)}, u32[]{:S(2)}, u32[]{:S(2)}) %collective-permute-start.3) | collective-permute-done | bytes 655392 | tf_op jit(solution)/shard_map/ppermute | solution.py:17
  149.2 9.6 %collective-permute-done.5 = bf16[256,1280]{1,0:T(8,128)(2,1)S(1)} collective-permute-done((bf16[256,1280]{1,0:T(8,128)(2,1)S(1)}, bf16[256,1280]{1,0:T(8,128)(2,1)S(1)}, u32[]{:S(2)}, u32[]{:S(2)}) %collective-permute-start.5) | collective-permute-done | bytes 655392 | tf_op jit(solution)/shard_map/ppermute | solution.py:17
  159.8 7.2 %copy.48 = bf16[1792,1280]{0,1:T(8,128)(2,1)} copy(bf16[1792,1280]{1,0:T(8,128)(2,1)} %constant_dynamic-update-slice_fusion) | data formatting | bytes 9175040 | tf_op jit(solution)/shard_map/concatenate | solution.py:55
  168.8 38.6 %collective-permute-done.10 = bf16[256,1280]{0,1:T(8,128)(2,1)S(1)} collective-permute-done((bf16[256,1280]{0,1:T(8,128)(2,1)S(1)}, bf16[256,1280]{0,1:T(8,128)(2,1)S(1)}, u32[]{:S(2)}, u32[]{:S(2)}) %collective-permute-start.10) | collective-permute-done | bytes 655392 | tf_op jit(solution)/shard_map/ppermute | solution.py:17
  210.4 12.0 %fusion.25 = (f32[10,256]{1,0:T(8,128)S(1)}, f32[10,256,1792]{1,2,0:T(8,128)}) fusion(pred[256,1792]{0,1:T(8,128)(4,1)} %compare_and_fusion, bf16[1792,10,128]{0,2,1:T(8,128)(2,1)} %bitcast.36, bf16[256,10,128]{0,2,1:T(8,128)(2,1)S(1)} %bitcast.33), kind=kOutput, calls=%fused_computation.61 | convolution fusion | flops 1192756992 | bytes 24061952 | tf_op jit(solution)/shard_map/sub | solution.py:69
  222.4 10.0 %fusion.12 = bf16[10,128,256]{2,1,0:T(8,128)(2,1)} fusion(bf16[1792,10,128]{0,2,1:T(8,128)(2,1)} %bitcast.32, f32[10,256,1792]{1,2,0:T(8,128)} %get-tuple-element.7, f32[10,256]{1,0:T(8,128)S(1)} %get-tuple-element.6), kind=kOutput, calls=%fused_computation.16 | convolution fusion | flops 1183907840 | bytes 23603200 | tf_op jit(solution)/shard_map/hqk,khd->qhd/dot_general | solution.py:71
  232.7 3.0 fusion.13
  235.8 10.3 %psum.21 = bf16[256,16]{0,1:T(8,128)(2,1)S(1)} all-reduce(f32[256,16]{0,1:T(8,128)S(1)} %fusion.13), channel_id=1, replica_groups=mesh['tok'=8,'hid'=4] {'hid'}, use_global_device_ids=true, to_apply=%region_8.9 | all-reduce | flops 4096 | bytes 24576 | tf_op jit(solution)/shard_map/psum | solution.py:94
  246.1 2.6 convolution_bitcast_fusion
  248.7 35.9 %all-gather.4.cloned.1.call-done = bf16[256,5120]{0,1:T(8,128)(2,1)} async-done(((bf16[256,1280]{0,1:T(8,128)(2,1)}), bf16[256,5120]{0,1:T(8,128)(2,1)}) %all-gather.4.cloned.1.call-update) | async-done | bytes 2621456 | tf_op jit(solution)/shard_map/all_gather | solution.py:74
  284.6 8.4 %fusion.26 = (f32[256]{0:T(256)S(1)}, f32[256,1280]{1,0:T(8,128)S(1)}) fusion(f32[256,1280]{1,0:T(8,128)S(1)} %convolution_bitcast_fusion, bf16[256,5120]{0,1:T(8,128)(2,1)} %all-gather.4.cloned.1.call-done, bf16[5120,1280]{1,0:T(8,128)(2,1)} %param.16, bf16[256,1280]{1,0:T(8,128)(2,1)S(1)} %copy-done), kind=kOutput, calls=%fused_computation.62 | convolution fusion | flops 3356753664 | bytes 19006464 | tf_op jit(solution)/shard_map/dot_general | solution.py:73
  293.0 5.9 %psum.22 = f32[256]{0:T(256)S(1)} all-reduce(f32[256]{0:T(256)S(1)} %get-tuple-element.8), channel_id=1, replica_groups=mesh['tok'=8,'hid'=4] {'hid'}, use_global_device_ids=true, to_apply=%region_10.11 | all-reduce | flops 256 | bytes 2048 | tf_op jit(solution)/shard_map/psum | solution.py:99
  299.2 5.7 %psum.23 = f32[256]{0:T(256)S(1)} all-reduce(f32[256]{0:T(256)S(1)} %multiply_reduce_fusion), channel_id=1, replica_groups=mesh['tok'=8,'hid'=4] {'hid'}, use_global_device_ids=true, to_apply=%region_12.13 | all-reduce | flops 256 | bytes 2048 | tf_op jit(solution)/shard_map/psum | solution.py:101
  (72 shorter events, 28.0 us)
Async XLA Ops:
  7.2 28.0 %copy-start.1 = (bf16[256,1280]{1,0:T(8,128)(2,1)S(1)}, bf16[256,1280]{1,0:T(8,128)(2,1)}, u32[]{:S(2)}) copy-start(bf16[256,1280]{1,0:T(8,128)(2,1)} %param.14) | copy-start | bytes 1966084
  7.2 225.5 %all-gather.6.cloned.1.call-start = ((), (), s32[]{:S(2)}) async-start(), calls=%async_computation.1 | async-start | bytes 2949120 | tf_op jit(solution)/shard_map/all_gather | solution.py:85
  7.9 238.2 %all-gather.8.cloned.1.call-start = ((), (), s32[]{:S(2)}) async-start(), calls=%async_computation.2 | async-start | bytes 2949120 | tf_op jit(solution)/shard_map/all_gather | solution.py:86
  9.3 26.8 %collective-permute-start.6 = (bf16[256,1280]{0,1:T(8,128)(2,1)S(1)}, bf16[256,1280]{0,1:T(8,128)(2,1)}, u32[]{:S(2)}, u32[]{:S(2)}) collective-permute-start(bf16[256,1280]{0,1:T(8,128)(2,1)S(1)} %copy.55), channel_id=1, source_target_pairs={{0,4},{4,8},{8,12},{12,16},{16,20},{20,24},{24,28},{1,5},{5,9},{9,... | collective-permute-start | bytes 1966088 | tf_op jit(solution)/shard_map/ppermute | solution.py:17
  15.0 50.0 %collective-permute-start.7 = (bf16[256,1280]{0,1:T(8,128)(2,1)S(1)}, bf16[256,1280]{0,1:T(8,128)(2,1)S(1)}, u32[]{:S(2)}, u32[]{:S(2)}) collective-permute-start(bf16[256,1280]{0,1:T(8,128)(2,1)S(1)} %copy.55), channel_id=1, source_target_pairs={{0,8},{4,12},{8,16},{12,20},{16,24},{20,28},{1,9},{5,13},{9,17},{1... | collective-permute-start | bytes 1966088 | tf_op jit(solution)/shard_map/ppermute | solution.py:17
  17.7 149.3 %collective-permute-start.8 = (bf16[256,1280]{0,1:T(8,128)(2,1)S(1)}, bf16[256,1280]{0,1:T(8,128)(2,1)S(1)}, u32[]{:S(2)}, u32[]{:S(2)}) collective-permute-start(bf16[256,1280]{0,1:T(8,128)(2,1)S(1)} %copy.55), channel_id=1, source_target_pairs={{0,12},{4,16},{8,20},{12,24},{16,28},{1,13},{5,17},{9,21},{13,25},... | collective-permute-start | bytes 1966088 | tf_op jit(solution)/shard_map/ppermute | solution.py:17
  22.1 145.8 %collective-permute-start.9 = (bf16[256,1280]{0,1:T(8,128)(2,1)S(1)}, bf16[256,1280]{0,1:T(8,128)(2,1)S(1)}, u32[]{:S(2)}, u32[]{:S(2)}) collective-permute-start(bf16[256,1280]{0,1:T(8,128)(2,1)S(1)} %copy.55), channel_id=1, source_target_pairs={{12,0},{16,4},{20,8},{24,12},{28,16},{13,1},{17,5},{21,9},{25,13},... | collective-permute-start | bytes 1966088 | tf_op jit(solution)/shard_map/ppermute | solution.py:17
  23.4 48.9 %collective-permute-start = (bf16[256,1280]{1,0:T(8,128)(2,1)}, bf16[256,1280]{1,0:T(8,128)(2,1)}, u32[]{:S(2)}, u32[]{:S(2)}) collective-permute-start(bf16[256,1280]{1,0:T(8,128)(2,1)} %param.14), channel_id=1, source_target_pairs={{0,4},{4,8},{8,12},{12,16},{16,20},{20,24},{24,28},{1,5},{5,9},{9,... | collective-permute-start | bytes 1966088 | tf_op jit(solution)/shard_map/ppermute | solution.py:17
  29.6 255.0 %all-gather.4.cloned.1.call-start = ((), (), s32[]{:S(2)}) async-start(), calls=%async_computation | async-start | bytes 3276800 | tf_op jit(solution)/shard_map/all_gather | solution.py:74
  36.0 56.9 %collective-permute-start.1 = (bf16[256,1280]{1,0:T(8,128)(2,1)S(1)}, bf16[256,1280]{1,0:T(8,128)(2,1)S(1)}, u32[]{:S(2)}, u32[]{:S(2)}) collective-permute-start(bf16[256,1280]{1,0:T(8,128)(2,1)S(1)} %copy-done.1), channel_id=1, source_target_pairs={{0,8},{4,12},{8,16},{12,20},{16,24},{20,28},{1,9},{5,13},{9,17},{1... | collective-permute-start | bytes 1966088 | tf_op jit(solution)/shard_map/ppermute | solution.py:17
  65.0 43.9 %collective-permute-start.2 = (bf16[256,1280]{1,0:T(8,128)(2,1)S(1)}, bf16[256,1280]{1,0:T(8,128)(2,1)S(1)}, u32[]{:S(2)}, u32[]{:S(2)}) collective-permute-start(bf16[256,1280]{1,0:T(8,128)(2,1)S(1)} %copy-done.1), channel_id=1, source_target_pairs={{0,12},{4,16},{8,20},{12,24},{16,28},{1,13},{5,17},{9,21},{13,25},... | collective-permute-start | bytes 1966088 | tf_op jit(solution)/shard_map/ppermute | solution.py:17
  70.2 2.1 copy-start.3
  72.4 72.5 %collective-permute-start.3 = (bf16[256,1280]{1,0:T(8,128)(2,1)S(1)}, bf16[256,1280]{1,0:T(8,128)(2,1)S(1)}, u32[]{:S(2)}, u32[]{:S(2)}) collective-permute-start(bf16[256,1280]{1,0:T(8,128)(2,1)S(1)} %copy-done.1), channel_id=1, source_target_pairs={{12,0},{16,4},{20,8},{24,12},{28,16},{13,1},{17,5},{21,9},{25,13},... | collective-permute-start | bytes 1966088 | tf_op jit(solution)/shard_map/ppermute | solution.py:17
  92.9 54.1 %collective-permute-start.4 = (bf16[256,1280]{1,0:T(8,128)(2,1)S(1)}, bf16[256,1280]{1,0:T(8,128)(2,1)S(1)}, u32[]{:S(2)}, u32[]{:S(2)}) collective-permute-start(bf16[256,1280]{1,0:T(8,128)(2,1)S(1)} %copy-done.1), channel_id=1, source_target_pairs={{8,0},{12,4},{16,8},{20,12},{24,16},{28,20},{9,1},{13,5},{17,9},{2... | collective-permute-start | bytes 1966088 | tf_op jit(solution)/shard_map/ppermute | solution.py:17
  108.9 50.0 %collective-permute-start.5 = (bf16[256,1280]{1,0:T(8,128)(2,1)S(1)}, bf16[256,1280]{1,0:T(8,128)(2,1)S(1)}, u32[]{:S(2)}, u32[]{:S(2)}) collective-permute-start(bf16[256,1280]{1,0:T(8,128)(2,1)S(1)} %copy-done.1), channel_id=1, source_target_pairs={{4,0},{8,4},{12,8},{16,12},{20,16},{24,20},{28,24},{5,1},{9,5},{13... | collective-permute-start | bytes 1966088 | tf_op jit(solution)/shard_map/ppermute | solution.py:17
  144.9 62.5 %collective-permute-start.10 = (bf16[256,1280]{0,1:T(8,128)(2,1)S(1)}, bf16[256,1280]{0,1:T(8,128)(2,1)S(1)}, u32[]{:S(2)}, u32[]{:S(2)}) collective-permute-start(bf16[256,1280]{0,1:T(8,128)(2,1)S(1)} %copy.55), channel_id=1, source_target_pairs={{8,0},{12,4},{16,8},{20,12},{24,16},{28,20},{9,1},{13,5},{17,9},{2... | collective-permute-start | bytes 1966088 | tf_op jit(solution)/shard_map/ppermute | solution.py:17
  147.1 61.3 %collective-permute-start.11 = (bf16[256,1280]{0,1:T(8,128)(2,1)S(1)}, bf16[256,1280]{0,1:T(8,128)(2,1)}, u32[]{:S(2)}, u32[]{:S(2)}) collective-permute-start(bf16[256,1280]{0,1:T(8,128)(2,1)S(1)} %copy.55), channel_id=1, source_target_pairs={{4,0},{8,4},{12,8},{16,12},{20,16},{24,20},{28,24},{5,1},{9,5},{13... | collective-permute-start | bytes 1966088 | tf_op jit(solution)/shard_map/ppermute | solution.py:17
  167.0 43.4 %copy-start.2 = (bf16[256,1280]{0,1:T(8,128)(2,1)S(1)}, bf16[256,1280]{0,1:T(8,128)(2,1)}, u32[]{:S(2)}) copy-start(bf16[256,1280]{0,1:T(8,128)(2,1)} %copy.56) | copy-start | bytes 1966084
  222.4 10.0 %copy-start.6 = (s32[64]{0:T(128)S(1)}, s32[64]{0:T(128)}, u32[]{:S(2)}) copy-start(s32[64]{0:T(128)} %param.21) | copy-start | bytes 772
  222.4 10.0 %copy-start.7 = (s32[4]{0:T(128)S(1)}, s32[4]{0:T(128)}, u32[]{:S(2)}) copy-start(s32[4]{0:T(128)} %param.20) | copy-start | bytes 52
  222.4 10.3 %copy-start.5 = (f32[1280]{0:T(1024)S(1)}, f32[1280]{0:T(1024)}, u32[]{:S(2)}) copy-start(f32[1280]{0:T(1024)} %param.22) | copy-start | bytes 15364
  232.7 51.9 %copy-start = (bf16[256,1280]{1,0:T(8,128)(2,1)S(1)}, bf16[256,1280]{1,0:T(8,128)(2,1)}, u32[]{:S(2)}) copy-start(bf16[256,1280]{1,0:T(8,128)(2,1)} %param.15) | copy-start | bytes 1966084
  248.7 56.2 %copy-start.4 = (f32[1280]{0:T(1024)S(1)}, f32[1280]{0:T(1024)}, u32[]{:S(2)}) copy-start(f32[1280]{0:T(1024)} %param.23) | copy-start | bytes 15364
Sparse Core Ops, SparseCore 0:
  10.2 90.4 all-gather.5
  102.9 100.3 all-gather.7
  232.5 52.0 all-gather.3
where the time goes:
time: 314 us; the launch traced here: 313 us
  waiting for transfers between devices  150 us (48%)
  starting transfers between devices  57.9 us (18%)
  matrix products  36 us (11%)
  local copies, waits for them, and re-layouts  28 us (9%)
  blocking collectives  21.9 us (7%)
  between operations  14.1 us (4%)
  other arithmetic  5.15 us (2%)
    ppermute x12, waiting for transfers between devices, shifted(): lax.ppermute(value, axis, [(source, source + steps) for source in range(i...  113 us
    ppermute x12, starting transfers between devices, shifted(): lax.ppermute(value, axis, [(source, source + steps) for source in range(i...  57.8 us
    all_gather x1, waiting for transfers between devices, on_device(): lax.all_gather(attended, 'hid', axis=1, tiled=True)  35.9 us
    unnamed x31, local copies, waits for them, and re-layouts  17.9 us
    sub x1, matrix products, on_device(): expo = jnp.exp(scores - top)  12 us
    psum x1, blocking collectives, on_device(): down = lax.psum(partial_down, 'hid').astype(jnp.bfloat16)  10.3 us
    dot_general x1, matrix products, on_device(): jnp.einsum('hqk,khd->qhd', weights, val_three, preferred_element_type=jnp...  9.96 us
    dot_general x1, matrix products, on_device(): jnp.dot(lax.all_gather(attended, 'hid', axis=1, tiled=True), out_weight,...  8.38 us
  transfers between devices with their start and end apart: 15, of which 6 were waited for; matrix products, arithmetic and copies ran while one was open for 18% of the time, Pallas kernels for 0%

commit v1 on v0

v1 whole, which is shorter than its diff:
```python
import functools
import math

import jax
import jax.numpy as jnp
from jax import lax
from jax.experimental import pallas as pl
from jax.experimental.pallas import tpu as pltpu
from jax.sharding import PartitionSpec as P

HEAD_DIM = 128
D = 5120
MESH = pl.DeviceIdType.MESH
NT = (((1,), (1,)), ((), ()))


def segment_of(pos, len_ref, requests):
    end = jnp.int32(0)
    seg = jnp.zeros_like(pos)
    for r in range(requests):
        end = end + len_ref[r]
        seg = seg + (pos >= end).astype(jnp.int32)
    return jnp.where(pos < 0, -1, seg)


def greet(targets):
    barrier = pltpu.get_barrier_semaphore()
    count = jnp.int32(0)
    for cond, dev in targets:

        def signal(dev=dev):
            pl.semaphore_signal(barrier, inc=1, device_id=dev, device_id_type=MESH)

        if cond is None:
            signal()
            count = count + 1
        else:
            pl.when(cond)(signal)
            count = count + cond.astype(jnp.int32)
    pl.semaphore_wait(barrier, count)


def run(cond, fn):
    if cond is None:
        fn()
    else:
        pl.when(cond)(fn)


def attention_kernel(
    n_tok, n_hid, requests,
    q_ref, k_ref, v_ref, w_ref, len_ref,
    acc_ref, att_ref,
    qb, kv, ag, wb, ob,
    w_sem, l_sem, ys, yr, zs, zr, ps, pr, fs, fr, as_, ar, hs, hr,
):
    rows, local = q_ref.shape
    hc = HEAD_DIM
    per = local // hc // 2
    tok, h = lax.axis_index("tok"), lax.axis_index("hid")
    p, y = tok // 2, tok % 2
    levels = n_tok // 2
    partner = (2 * p + 1 - y, h)
    up, down = (tok + 2, h), (tok - 2, h)
    has_up, has_down = p < levels - 1, p > 0
    others = [(tok, lax.rem(h + d, n_hid)) for d in range(1, n_hid)]
    greet([(None, partner), (has_up, up), (has_down, down)] + [(None, o) for o in others])

    own = pl.multiple_of(y * rows, rows)
    oth = pl.multiple_of((1 - y) * rows, rows)
    own_cols = y * (per * hc)
    oth_cols = (1 - y) * (per * hc)
    base = 3 * rows
    sends = []

    def remote(src, dst, ss, rs, dev):
        return pltpu.make_async_remote_copy(
            src_ref=src, dst_ref=dst, send_sem=ss, recv_sem=rs, device_id=dev, device_id_type=MESH
        )

    def go(cond, copy):
        run(cond, lambda: copy.start())
        sends.append((cond, copy))

    def cols(start, j):
        return pl.ds(pl.multiple_of(start + j * hc, hc), hc)

    ways = [(has_up, up, base - 2 * rows, has_down), (has_down, down, base + 2 * rows, has_up)]

    y_copies, l_copies, z_copies = [], [], []
    for j in range(per):
        yc, lc, zc = [], [], []
        for i, (ref, at) in enumerate(((k_ref, kv), (v_ref, kv), (q_ref, qb))):
            src = ref.at[:, cols(oth_cols, j)]
            mine = ref.at[:, cols(own_cols, j)]
            dst = kv.at[j, i, pl.ds(base + own, rows), :] if i < 2 else qb.at[j, pl.ds(own, rows), :]
            c = remote(src, dst, ys.at[j, i], yr.at[j, i], partner)
            go(None, c)
            yc.append(c)
            c = pltpu.make_async_copy(mine, dst, l_sem.at[j, i])
            c.start()
            lc.append(c)
            if i < 2:
                for w, (cond, dev, first, rcond) in enumerate(ways):
                    c = remote(
                        mine, kv.at[j, i, pl.ds(first + own, rows), :], zs.at[j, w, i], zr.at[j, w, i], dev
                    )
                    go(cond, c)
                    zc.append((rcond, c))
        y_copies.append(yc)
        l_copies.append(lc)
        z_copies.append(zc)

    w_copies = []
    for j in range(per):
        wc = []
        for g in range(2 * n_hid):
            row = (g // 2) * local + (g % 2) * per * hc + j * hc
            c = pltpu.make_async_copy(
                w_ref.at[pl.ds(row, hc), :], wb.at[j, pl.ds(g * hc, hc), :], w_sem.at[j, g]
            )
            c.start()
            wc.append(c)
        w_copies.append(wc)

    @pl.when(p == 0)
    def _():
        kv[:, :, 0 : 3 * rows, :] = jnp.zeros((per, 2, 3 * rows, hc), kv.dtype)

    @pl.when(p == 1)
    def _():
        kv[:, :, 0:rows, :] = jnp.zeros((per, 2, rows, hc), kv.dtype)

    @pl.when(p == levels - 1)
    def _():
        kv[:, :, 5 * rows : 8 * rows, :] = jnp.zeros((per, 2, 3 * rows, hc), kv.dtype)

    @pl.when(p == levels - 2)
    def _():
        kv[:, :, 7 * rows : 8 * rows, :] = jnp.zeros((per, 2, rows, hc), kv.dtype)

    p_copies = []

    def stage_a(j):
        for c in y_copies[j]:
            c.wait_recv()
        pc = []
        for w, (cond, dev, first, rcond) in enumerate(ways):
            c = remote(
                kv.at[j, :, pl.ds(base + oth, rows), :],
                kv.at[j, :, pl.ds(first + oth, rows), :],
                ps.at[j, w], pr.at[j, w], dev,
            )
            go(cond, c)
            pc.append((rcond, c))
        p_copies.append(pc)

    f_copies = []
    fwd = [
        (has_up & has_down, up, 2 * rows, 0, p > 1),
        (has_up & has_down, down, 5 * rows, 7 * rows, p < levels - 2),
    ]

    def stage_b(j):
        fc = []
        for w, (cond, dev, src, dst, rcond) in enumerate(fwd):
            for rc, c in z_copies[j][w::2] + p_copies[j][w : w + 1]:
                run(rc, lambda c=c: c.wait_recv())
            c = remote(
                kv.at[j, :, pl.ds(src, rows), :], kv.at[j, :, pl.ds(dst, rows), :],
                fs.at[j, w], fr.at[j, w], dev,
            )
            go(cond, c)
            fc.append((rcond, c))
        f_copies.append(fc)

    scale = math.log2(math.e) / math.sqrt(HEAD_DIM)
    tile = 128
    span = 7 * rows

    def attend(j, first, store):
        level_pos = p * (2 * rows)
        kseg = segment_of(
            level_pos - base + first + lax.broadcasted_iota(jnp.int32, (1, span), 1), len_ref, requests
        )

        def body(t, carry):
            at = pl.multiple_of(t * tile, tile)
            qseg = segment_of(
                level_pos + first + at + lax.broadcasted_iota(jnp.int32, (tile, 1), 0), len_ref, requests
            )
            q = qb[j, pl.ds(first + at, tile), :]
            s = lax.dot_general(
                q, kv[j, 0, pl.ds(first, span), :], NT, preferred_element_type=jnp.float32
            )
            s = jnp.where(qseg == kseg, s, -1e30)
            top = jnp.max(s, axis=1, keepdims=True)
            e = jnp.exp2((s - top) * scale)
            total = jnp.sum(e, axis=1, keepdims=True)
            o = jnp.dot(
                e.astype(jnp.bfloat16), kv[j, 1, pl.ds(first, span), :], preferred_element_type=jnp.float32
            )
            store(at, (o / total).astype(jnp.bfloat16))
            return carry

        lax.fori_loop(0, rows // tile, body, 0)

    a_copies = []
    my_col = pl.ds(pl.multiple_of((h * 2 + y) * hc, hc), hc)

    def stage_c(j):
        for c in l_copies[j]:
            c.wait()
        for rc, c in f_copies[j]:
            run(rc, lambda c=c: c.wait_recv())

        def store_other(at, o):
            ob[j, pl.ds(at, tile), :] = o

        def store_own(at, o):
            ag[j, pl.ds(at, tile), my_col] = o

        attend(j, oth, store_other)
        c = remote(ob.at[j], ag.at[j, :, my_col], as_.at[j], ar.at[j], partner)
        go(None, c)
        a_copies.append(c)
        attend(j, own, store_own)

    h_copies = []
    pair_cols = pl.ds(pl.multiple_of(h * 2 * hc, 2 * hc), 2 * hc)

    def stage_d(j):
        a_copies[j].wait_recv()
        hcs = []
        for d, dev in enumerate(others):
            c = remote(ag.at[j, :, pair_cols], ag.at[j, :, pair_cols], hs.at[j, d], hr.at[j, d], dev)
            go(None, c)
            hcs.append(c)
        h_copies.append(hcs)
        pair = ag[j, :, pair_cols]
        att_ref[:, j * hc : (j + 1) * hc] = pair[:, :hc]
        att_ref[:, (per + j) * hc : (per + j + 1) * hc] = pair[:, hc:]

    def stage_e(j):
        for c in h_copies[j]:
            c.wait_recv()
        for c in w_copies[j]:
            c.wait()

        def body(t, carry):
            n = pl.ds(pl.multiple_of(t * 256, 256), 256)
            part = jnp.dot(ag[j], wb[j, :, n], preferred_element_type=jnp.float32)
            if j == 0:
                acc_ref[:, n] = part
            else:
                acc_ref[:, n] += part
            return carry

        lax.fori_loop(0, local // 256, body, 0)

    stages = [stage_a, stage_b, stage_c, stage_d, stage_e]
    for step in range(per + len(stages) - 1):
        for i, stage in enumerate(stages):
            if 0 <= step - i < per:
                stage(step - i)
    for cond, c in sends:
        run(cond, lambda c=c: c.wait_send())


def attention(q, k, v, w, lengths):
    n_tok, n_hid = lax.axis_size("tok"), lax.axis_size("hid")
    rows, local = q.shape
    per = local // HEAD_DIM // 2
    dma = pltpu.SemaphoreType.DMA
    any_ = pl.BlockSpec(memory_space=pl.ANY)
    vm = pl.BlockSpec(memory_space=pltpu.VMEM)
    bf = jnp.bfloat16
    return pl.pallas_call(
        functools.partial(attention_kernel, n_tok, n_hid, lengths.shape[0]),
        out_shape=(
            jax.ShapeDtypeStruct((rows, local), jnp.float32),
            jax.ShapeDtypeStruct((rows, local), bf),
        ),
        in_specs=[any_] * 4 + [pl.BlockSpec(memory_space=pltpu.SMEM)],
        out_specs=(vm, vm),
        scratch_shapes=[
            pltpu.VMEM((per, 2 * rows, HEAD_DIM), bf),
            pltpu.VMEM((per, 2, 8 * rows, HEAD_DIM), bf),
            pltpu.VMEM((per, rows, 2 * n_hid * HEAD_DIM), bf),
            pltpu.VMEM((per, 2 * n_hid * HEAD_DIM, local), bf),
            pltpu.VMEM((per, rows, HEAD_DIM), bf),
            dma((per, 2 * n_hid)),
            dma((per, 3)),
            dma((per, 3)),
            dma((per, 3)),
            dma((per, 2, 2)),
            dma((per, 2, 2)),
            dma((per, 2)),
            dma((per, 2)),
            dma((per, 2)),
            dma((per, 2)),
            dma((per,)),
            dma((per,)),
            dma((per, n_hid - 1)),
            dma((per, n_hid - 1)),
        ],
        compiler_params=pltpu.CompilerParams(
            collective_id=0, has_side_effects=True, vmem_limit_bytes=44 * 1024 * 1024
        ),
        cost_estimate=pl.CostEstimate(
            flops=6_000_000_000, bytes_accessed=200_000_000, transcendentals=5_000_000
        ),
        name="attention_project",
    )(q, k, v, w, lengths)


def finish_kernel(
    n_hid, requests, rank,
    acc_ref, att_ref, res_ref, maps_ref, scale_ref, shift_ref, len_ref,
    stream_ref, normed_ref,
    tot, db, sb, ds_, dr, ss_, sr,
):
    rows, local = acc_ref.shape
    tok, h = lax.axis_index("tok"), lax.axis_index("hid")
    others = [(tok, lax.rem(h + d, n_hid)) for d in range(1, n_hid)]
    greet([(None, o) for o in others])
    wide = requests * rank

    def exchange(buf, ssem, rsem):
        copies = []
        for d, dev in enumerate(others):
            c = pltpu.make_async_remote_copy(
                src_ref=buf.at[h], dst_ref=buf.at[h], send_sem=ssem.at[d], recv_sem=rsem.at[d],
                device_id=dev, device_id_type=MESH,
            )
            c.start()
            copies.append(c)
        return copies

    seg = segment_of(tok * rows + lax.broadcasted_iota(jnp.int32, (1, rows), 1), len_ref, requests)
    mine = lax.broadcasted_iota(jnp.int32, (wide, rows), 0) // rank == seg
    part = lax.dot_general(maps_ref[0:wide, :], att_ref[...], NT, preferred_element_type=jnp.float32)
    part = jnp.where(mine, part, 0.0)
    folded = part[0:rank, :]
    for r in range(1, requests):
        folded = folded + part[r * rank : (r + 1) * rank, :]
    db[h] = folded
    copies = exchange(db, ds_, dr)
    tot[...] = acc_ref[...] + res_ref[...].astype(jnp.float32)
    for c in copies:
        c.wait()
    down = db[0]
    for g in range(1, n_hid):
        down = down + db[g]
    down = jnp.concatenate([down] * requests, axis=0)
    expand = jnp.where(mine, down, 0.0).astype(jnp.bfloat16)
    lift = lax.dot_general(
        expand, maps_ref[wide : 2 * wide, :], (((0,), (0,)), ((), ())), preferred_element_type=jnp.float32
    )
    total = tot[...] + lift
    tot[...] = total
    mean = jnp.sum(total, axis=1, keepdims=True) / local
    off = total - mean
    square = jnp.sum(off * off, axis=1, keepdims=True)
    lane = lax.broadcasted_iota(jnp.int32, (rows, 128), 1)
    sb[h] = jnp.transpose(jnp.where(lane == 0, mean, square))[0:8, :]
    copies = exchange(sb, ss_, sr)
    stream_ref[...] = total.astype(jnp.bfloat16)
    for c in copies:
        c.wait()
    stats = [sb[g] for g in range(n_hid)]
    means = [s[0:1, :] for s in stats]
    mean = sum(means[1:], means[0]) / n_hid
    var = stats[0][1:2, :] + local * (means[0] - mean) * (means[0] - mean)
    for g in range(1, n_hid):
        var = var + stats[g][1:2, :] + local * (means[g] - mean) * (means[g] - mean)
    inv = 1.0 / jnp.sqrt(var / (local * n_hid) + 1e-06)
    row = lax.broadcasted_iota(jnp.int32, (128, rows), 0)
    back = jnp.transpose(jnp.where(row == 0, mean, inv))
    normed_ref[...] = (
        (tot[...] - back[:, 0:1]) * back[:, 1:2] * (1.0 + scale_ref[...]) + shift_ref[...]
    ).astype(jnp.bfloat16)


def finish(acc, att, residual, maps, scale, shift, lengths, rank):
    n_hid = lax.axis_size("hid")
    rows, local = acc.shape
    dma = pltpu.SemaphoreType.DMA
    vm = pl.BlockSpec(memory_space=pltpu.VMEM)
    return pl.pallas_call(
        functools.partial(finish_kernel, n_hid, lengths.shape[0], rank),
        out_shape=(jax.ShapeDtypeStruct((rows, local), jnp.bfloat16),) * 2,
        in_specs=[vm] * 6 + [pl.BlockSpec(memory_space=pltpu.SMEM)],
        out_specs=(vm, vm),
        scratch_shapes=[
            pltpu.VMEM((rows, local), jnp.float32),
            pltpu.VMEM((n_hid, rank, rows), jnp.float32),
            pltpu.VMEM((n_hid, 8, rows), jnp.float32),
            dma((n_hid - 1,)),
            dma((n_hid - 1,)),
            dma((n_hid - 1,)),
            dma((n_hid - 1,)),
        ],
        compiler_params=pltpu.CompilerParams(
            collective_id=1, has_side_effects=True, vmem_limit_bytes=32 * 1024 * 1024
        ),
        name="adapter_norm",
    )(acc, att, residual, maps, scale, shift, lengths)


def on_device(
    queries, keys, values, residual, out_weight, adapter_a, adapter_b,
    request_lengths, request_adapter, adapter_slot, mod_scale, mod_shift,
):
    held, local, rank = adapter_a.shape
    requests = request_lengths.shape[0]
    slots = adapter_slot[request_adapter] - lax.axis_index("tok") * held
    here = ((slots >= 0) & (slots < held))[:, None, None]
    slots = jnp.clip(slots, 0, held - 1)
    take = lambda bank: jnp.stack(
        [lax.dynamic_index_in_dim(bank, slots[r], 0, keepdims=False) for r in range(requests)]
    )
    a = jnp.where(here, jnp.transpose(take(adapter_a), (0, 2, 1)), 0)
    b = jnp.where(here, take(adapter_b), 0)
    maps = jnp.concatenate([a.reshape(requests * rank, local), b.reshape(requests * rank, local)], axis=0)
    maps = lax.psum(maps, "tok")
    acc, att = attention(queries, keys, values, out_weight, request_lengths)
    return finish(acc, att, residual, maps, mod_scale[None, :], mod_shift[None, :], request_lengths, rank)


def solution(mesh):
    placed = (
        P("tok", "hid"),
        P("tok", "hid"),
        P("tok", "hid"),
        P("tok", "hid"),
        P(None, "hid"),
        P("tok", "hid", None),
        P("tok", None, "hid"),
        P(),
        P(),
        P(),
        P("hid"),
        P("hid"),
    )
    return jax.shard_map(
        on_device,
        mesh=mesh,
        in_specs=placed,
        out_specs=(P("tok", "hid"), P("tok", "hid")),
        check_vma=False,
    )
```

time: 314 us -> 119 us (0.38)
  waiting for transfers between devices: 150 us -> 0.04 us
  Pallas kernels: 0 us -> 83.6 us
  starting transfers between devices: 57.9 us -> 0.04 us
  matrix products: 36 us -> 0 us
  blocking collectives: 21.9 us -> 0 us
  local copies, waits for them, and re-layouts: 28 us -> 11.3 us
  between operations: 14.1 us -> 21.6 us
  other arithmetic: 5.15 us -> 1.68 us
    ppermute x12 -> x0, waiting for transfers between devices: 113 us -> none  [shifted(): lax.ppermute(value, axis, [(source, source + steps) for source in range(i...]
    pallas_call x0 -> x2, Pallas kernels: none -> 83.6 us  [the longest x1 72.8 us: attention(): pl.pallas_call(functools.partial(attention_kernel, n_tok, n_hid, lengths....]
    ppermute x12 -> x0, starting transfers between devices: 57.8 us -> none  [shifted(): lax.ppermute(value, axis, [(source, source + steps) for source in range(i...]
    all_gather x3 -> x0, waiting for transfers between devices: 35.9 us -> none  [the longest x1 35.9 us: on_device(): lax.all_gather(attended, 'hid', axis=1, tiled=True)]
    dot_general x4 -> x0, matrix products: 24 us -> none  [the longest x1 9.96 us: on_device(): jnp.einsum('hqk,khd->qhd', weights, val_three, preferred_element_type=jnp...]
    psum x3 -> x0, blocking collectives: 21.9 us -> none  [the longest x1 10.3 us: on_device(): down = lax.psum(partial_down, 'hid').astype(jnp.bfloat16)]
    sub x1 -> x0, matrix products: 12 us -> none  [on_device(): expo = jnp.exp(scores - top)]
    unnamed x31 -> x18, local copies, waits for them, and re-layouts: 17.9 us -> 6.58 us
  transfers between devices with their start and end apart: 15 -> 1, of which waited for: 6 -> 0; matrix products, arithmetic and copies ran while one was open for 18% -> 1% of each run, Pallas kernels for 0% -> 62%
where the time goes in v1:
time: 119 us; the launch traced here: 118 us
  Pallas kernels  83.6 us (70%)
  between operations  21.6 us (18%)
  local copies, waits for them, and re-layouts  11.3 us (9%)
  other arithmetic  1.68 us (1%)
    pallas_call x1, Pallas kernels, attention(): pl.pallas_call(functools.partial(attention_kernel, n_tok, n_hid, lengths....  72.8 us
    pallas_call x1, Pallas kernels, finish(): pl.pallas_call(functools.partial(finish_kernel, n_hid, lengths.shape[0],...  10.8 us
    unnamed x18, local copies, waits for them, and re-layouts  6.58 us
  transfers between devices with their start and end apart: 1, of which 0 were waited for; matrix products, arithmetic and copies ran while one was open for 1% of the time, Pallas kernels for 62%

profile of v1, /device:TPU:0, one launch (start us, length us, event | category | flops | bytes accessed | tf_op | source)
XLA Modules:
  0.0 118.2 jit_solution(15628939083151816383)
XLA Ops:
  7.2 0.0 all-reduce.2.cloned.1.call-start
  7.3 0.7 compare_select_fusion
  8.0 0.6 gather_fusion
  8.6 0.6 fusion
  14.2 0.1 broadcast_in_dim.37
  14.3 0.1 broadcast_in_dim.38
  16.9 0.9 constant_dynamic-slice_fusion.3
  17.8 1.0 constant_dynamic-slice_fusion.7
  18.8 0.1 bitcast_select_fusion
  18.9 0.1 maximum_select_fusion
  19.0 0.7 pad_maximum_fusion
  19.8 0.0 all-reduce.2.cloned.1.call-update
  19.8 0.7 broadcast_in_dim.41.scale_ref
  20.5 0.7 broadcast_in_dim.42.shift_ref
  21.2 0.7 copy-done.3
  21.9 1.1 copy-done.5
  22.9 1.1 copy-done.6
  24.0 1.1 copy-done.7
  25.1 72.8 %attention_project.1 = (f32[256,1280]{1,0:T(8,128)S(1)}, bf16[256,1280]{1,0:T(8,128)(2,1)S(1)}) custom-call(bf16[256,1280]{1,0:T(8,128)(2,1)S(1)} %copy-done.5, bf16[256,1280]{1,0:T(8,128)(2,1)S(1)} %copy-done.6, bf16[256,1280]{1,0:T(8,128)(2,1)S(1)} %copy-done.7, bf16[5120,1280]{1,0:T(8,128)(2,1)} %w_ref.1, s32[4]{0:T(128)S(1)} %copy-done.3), custom_call_target="tpu_custom_call" | custom-call | flops 6000000000 | bytes 200000000 | tf_op jit(solution)/shard_map/attention_project/pallas_call | solution.py:278
  97.9 0.0 all-reduce.2.cloned.1.call-done.maps_ref
  97.9 1.0 copy-done.2
  98.9 10.8 %adapter_norm.1 = (bf16[256,1280]{1,0:T(8,128)(2,1)S(1)}, bf16[256,1280]{1,0:T(8,128)(2,1)S(1)}) custom-call(f32[256,1280]{1,0:T(8,128)S(1)} %get-tuple-element.4.acc_ref, bf16[256,1280]{1,0:T(8,128)(2,1)S(1)} %get-tuple-element.5.att_ref, bf16[256,1280]{1,0:T(8,128)(2,1)S(1)} %copy-done.1, bf16[128,1280]{1,0:T(8,128)(2,1)S(1)} %copy-done.2, ...), custom_call_target="tpu_custom_call" | custom-call | tf_op jit(solution)/shard_map/adapter_norm/pallas_call | solution.py:390
  109.7 0.8 copy.17
  110.5 0.8 copy.18
  (15 shorter events, 0.1 us)
Async XLA Ops:
  7.2 0.8 copy-start
  7.2 90.7 %copy-start.4 = (s32[4]{0:T(128)S(1)}, s32[4]{0:T(128)}, u32[]{:S(2)}) copy-start(s32[4]{0:T(128)} %len_ref.3) | copy-start | bytes 52
  7.2 90.7 %copy-start.1 = (bf16[256,1280]{1,0:T(8,128)(2,1)S(1)}, bf16[256,1280]{1,0:T(8,128)(2,1)}, u32[]{:S(2)}) copy-start(bf16[256,1280]{1,0:T(8,128)(2,1)} %res_ref.1) | copy-start | bytes 1966084
  7.2 90.7 %all-reduce.2.cloned.1.call-start = ((), (), s32[]{:S(2)}) async-start(), calls=%async_computation | async-start | bytes 655360 | tf_op jit(solution)/shard_map/psum | solution.py:426
  21.2 0.7 copy-start.3
  21.9 1.1 copy-start.5
  22.9 1.1 copy-start.6
  24.0 1.1 copy-start.7
  97.9 1.0 copy-start.2
Sparse Core Ops, SparseCore 0:
  19.9 75.5 all-reduce.1

commit v2 on v1

--- a/solution.py
+++ b/solution.py
@@ -47,16 +47,18 @@
         pl.when(cond)(fn)
 
 
-def attention_kernel(
-    n_tok, n_hid, requests,
-    q_ref, k_ref, v_ref, w_ref, len_ref,
-    acc_ref, att_ref,
-    qb, kv, ag, wb, ob,
-    w_sem, l_sem, ys, yr, zs, zr, ps, pr, fs, fr, as_, ar, hs, hr,
+def block_kernel(
+    n_tok, n_hid, requests, rank,
+    q_ref, k_ref, v_ref, w_ref, res_ref, a_ref, b_ref, scale_ref, shift_ref, len_ref, req_ref, slot_ref,
+    stream_ref, normed_ref,
+    qb, kv, ag, wb, ob, acc_ref, att_ref, mo, mi, cu, cd, fu, fd, tm, db, sb,
+    w_sem, l_sem, ys, yr, zs, zr, ps, pr, fs, fr, as_, ar, hs, hr, ms, mr, ds_, dr, ss_, sr,
 ):
     rows, local = q_ref.shape
     hc = HEAD_DIM
-    per = local // hc // 2
+    heads = local // hc
+    per = (heads + 1) // 2
+    second = heads - per
     tok, h = lax.axis_index("tok"), lax.axis_index("hid")
     p, y = tok // 2, tok % 2
     levels = n_tok // 2
@@ -68,8 +70,8 @@
 
     own = pl.multiple_of(y * rows, rows)
     oth = pl.multiple_of((1 - y) * rows, rows)
-    own_cols = y * (per * hc)
-    oth_cols = (1 - y) * (per * hc)
+    own_cols = y * (second * hc)
+    oth_cols = (1 - y) * (second * hc)
     base = 3 * rows
     sends = []
 
@@ -86,6 +88,55 @@
         return pl.ds(pl.multiple_of(start + j * hc, hc), hc)
 
     ways = [(has_up, up, base - 2 * rows, has_down), (has_down, down, base + 2 * rows, has_up)]
+
+    wide = requests * rank
+    held = a_ref.shape[0]
+    for i, bank in enumerate((a_ref, b_ref)):
+        for r in range(requests):
+            slot = slot_ref[req_ref[r]] - tok * held
+            held_here = (slot >= 0) & (slot < held)
+            got = bank[jnp.clip(slot, 0, held - 1)]
+            mo[i, r * rank : (r + 1) * rank, :] = jnp.where(held_here, got, jnp.zeros_like(got))
+    m_pair = remote(mo.at[1 - y], mi, ms.at[0], mr.at[0], partner)
+    m_up = remote(fu, cu, ms.at[1], mr.at[1], up)
+    m_down = remote(fd, cd, ms.at[2], mr.at[2], down)
+    m_back = remote(tm.at[y], tm.at[y], ms.at[3], mr.at[3], partner)
+
+    @pl.when(p == 0)
+    def _():
+        cu[...] = jnp.zeros_like(cu)
+
+    @pl.when(p == levels - 1)
+    def _():
+        cd[...] = jnp.zeros_like(cd)
+
+    chain_steps = 4
+
+    def maps_at(step):
+        if step == 0:
+            m_pair.wait_recv()
+            mi[...] = mi[...] + mo[y]
+        if step < chain_steps:
+            back = levels - 1 - p
+            last = step == chain_steps - 1
+
+            @pl.when((p >= step) if last else (p == step))
+            def _():
+                run(has_down, lambda: m_up.wait_recv())
+                fu[...] = mi[...] + cu[...]
+                run(has_up, lambda: m_up.start())
+
+            @pl.when((back >= step) if last else (back == step))
+            def _():
+                run(has_up, lambda: m_down.wait_recv())
+                fd[...] = mi[...] + cd[...]
+                run(has_down, lambda: m_down.start())
+
+        if step == chain_steps:
+            tm[y] = mi[...] + cu[...] + cd[...]
+            m_back.start()
+
+    sends.extend([(None, m_pair), (has_up, m_up), (has_down, m_down), (None, m_back)])
 
     y_copies, l_copies, z_copies = [], [], []
     for j in range(per):
@@ -111,11 +162,15 @@
         l_copies.append(lc)
         z_copies.append(zc)
 
+    m_pair.start()
     w_copies = []
     for j in range(per):
         wc = []
         for g in range(2 * n_hid):
-            row = (g // 2) * local + (g % 2) * per * hc + j * hc
+            row = (g // 2) * local + (g % 2) * second * hc + j * hc
+            if g % 2 == 1 and j < per - second:
+                wb[j, g * hc : (g + 1) * hc, :] = jnp.zeros((hc, local), wb.dtype)
+                continue
             c = pltpu.make_async_copy(
                 w_ref.at[pl.ds(row, hc), :], wb.at[j, pl.ds(g * hc, hc), :], w_sem.at[j, g]
             )
@@ -174,6 +229,7 @@
             fc.append((rcond, c))
         f_copies.append(fc)
 
+    wide_tile = 256 if local % 256 == 0 else 128
     scale = math.log2(math.e) / math.sqrt(HEAD_DIM)
     tile = 128
     span = 7 * rows
@@ -226,29 +282,44 @@
         a_copies.append(c)
         attend(j, own, store_own)
 
-    h_copies = []
+    h_copies, t_copies = [], []
+    x, core, nx = h // 2, h % 2, n_hid // 2
+    twin = (tok, x * 2 + 1 - core)
     pair_cols = pl.ds(pl.multiple_of(h * 2 * hc, 2 * hc), 2 * hc)
 
     def stage_d(j):
         a_copies[j].wait_recv()
         hcs = []
-        for d, dev in enumerate(others):
+        for d in range(1, nx):
+            dev = (tok, lax.rem(x + d, nx) * 2 + core)
             c = remote(ag.at[j, :, pair_cols], ag.at[j, :, pair_cols], hs.at[j, d], hr.at[j, d], dev)
             go(None, c)
             hcs.append(c)
+        c = remote(ag.at[j, :, pair_cols], ag.at[j, :, pair_cols], hs.at[j, 0], hr.at[j, 0], twin)
+        go(None, c)
         h_copies.append(hcs)
+        t_copies.append([c])
         pair = ag[j, :, pair_cols]
         att_ref[:, j * hc : (j + 1) * hc] = pair[:, :hc]
-        att_ref[:, (per + j) * hc : (per + j + 1) * hc] = pair[:, hc:]
+        att_ref[:, (second + j) * hc : (second + j + 1) * hc] = pair[:, hc:]
+
+    def stage_t(j):
+        for d in range(1, nx):
+            h_copies[j][d - 1].wait_recv()
+            there = lax.rem(x - d + nx, nx) * 2 + core
+            at = pl.ds(pl.multiple_of(there * 2 * hc, 2 * hc), 2 * hc)
+            c = remote(ag.at[j, :, at], ag.at[j, :, at], hs.at[j, nx - 1 + d], hr.at[j, nx - 1 + d], twin)
+            go(None, c)
+            t_copies[j].append(c)
 
     def stage_e(j):
-        for c in h_copies[j]:
+        for c in t_copies[j]:
             c.wait_recv()
         for c in w_copies[j]:
             c.wait()
 
         def body(t, carry):
-            n = pl.ds(pl.multiple_of(t * 256, 256), 256)
+            n = pl.ds(pl.multiple_of(t * wide_tile, wide_tile), wide_tile)
             part = jnp.dot(ag[j], wb[j, :, n], preferred_element_type=jnp.float32)
             if j == 0:
                 acc_ref[:, n] = part
@@ -256,75 +327,7 @@
                 acc_ref[:, n] += part
             return carry
 
-        lax.fori_loop(0, local // 256, body, 0)
-
-    stages = [stage_a, stage_b, stage_c, stage_d, stage_e]
-    for step in range(per + len(stages) - 1):
-        for i, stage in enumerate(stages):
-            if 0 <= step - i < per:
-                stage(step - i)
-    for cond, c in sends:
-        run(cond, lambda c=c: c.wait_send())
-
-
-def attention(q, k, v, w, lengths):
-    n_tok, n_hid = lax.axis_size("tok"), lax.axis_size("hid")
-    rows, local = q.shape
-    per = local // HEAD_DIM // 2
-    dma = pltpu.SemaphoreType.DMA
-    any_ = pl.BlockSpec(memory_space=pl.ANY)
-    vm = pl.BlockSpec(memory_space=pltpu.VMEM)
-    bf = jnp.bfloat16
-    return pl.pallas_call(
-        functools.partial(attention_kernel, n_tok, n_hid, lengths.shape[0]),
-        out_shape=(
-            jax.ShapeDtypeStruct((rows, local), jnp.float32),
-            jax.ShapeDtypeStruct((rows, local), bf),
-        ),
-        in_specs=[any_] * 4 + [pl.BlockSpec(memory_space=pltpu.SMEM)],
-        out_specs=(vm, vm),
-        scratch_shapes=[
-            pltpu.VMEM((per, 2 * rows, HEAD_DIM), bf),
-            pltpu.VMEM((per, 2, 8 * rows, HEAD_DIM), bf),
-            pltpu.VMEM((per, rows, 2 * n_hid * HEAD_DIM), bf),
-            pltpu.VMEM((per, 2 * n_hid * HEAD_DIM, local), bf),
-            pltpu.VMEM((per, rows, HEAD_DIM), bf),
-            dma((per, 2 * n_hid)),
-            dma((per, 3)),
-            dma((per, 3)),
-            dma((per, 3)),
-            dma((per, 2, 2)),
-            dma((per, 2, 2)),
-            dma((per, 2)),
-            dma((per, 2)),
-            dma((per, 2)),
-            dma((per, 2)),
-            dma((per,)),
-            dma((per,)),
-            dma((per, n_hid - 1)),
-            dma((per, n_hid - 1)),
-        ],
-        compiler_params=pltpu.CompilerParams(
-            collective_id=0, has_side_effects=True, vmem_limit_bytes=44 * 1024 * 1024
-        ),
-        cost_estimate=pl.CostEstimate(
-            flops=6_000_000_000, bytes_accessed=200_000_000, transcendentals=5_000_000
-        ),
-        name="attention_project",
-    )(q, k, v, w, lengths)
-
-
-def finish_kernel(
-    n_hid, requests, rank,
-    acc_ref, att_ref, res_ref, maps_ref, scale_ref, shift_ref, len_ref,
-    stream_ref, normed_ref,
-    tot, db, sb, ds_, dr, ss_, sr,
-):
-    rows, local = acc_ref.shape
-    tok, h = lax.axis_index("tok"), lax.axis_index("hid")
-    others = [(tok, lax.rem(h + d, n_hid)) for d in range(1, n_hid)]
-    greet([(None, o) for o in others])
-    wide = requests * rank
+        lax.fori_loop(0, local // wide_tile, body, 0)
 
     def exchange(buf, ssem, rsem):
         copies = []
@@ -337,16 +340,26 @@
             copies.append(c)
         return copies
 
-    seg = segment_of(tok * rows + lax.broadcasted_iota(jnp.int32, (1, rows), 1), len_ref, requests)
-    mine = lax.broadcasted_iota(jnp.int32, (wide, rows), 0) // rank == seg
-    part = lax.dot_general(maps_ref[0:wide, :], att_ref[...], NT, preferred_element_type=jnp.float32)
-    part = jnp.where(mine, part, 0.0)
-    folded = part[0:rank, :]
-    for r in range(1, requests):
-        folded = folded + part[r * rank : (r + 1) * rank, :]
-    db[h] = folded
-    copies = exchange(db, ds_, dr)
-    tot[...] = acc_ref[...] + res_ref[...].astype(jnp.float32)
+    def adapter_down():
+        seg = segment_of(tok * rows + lax.broadcasted_iota(jnp.int32, (1, rows), 1), len_ref, requests)
+        mine = lax.broadcasted_iota(jnp.int32, (wide, rows), 0) // rank == seg
+        part = lax.dot_general(tm[0], att_ref[...], NT, preferred_element_type=jnp.float32)
+        part = jnp.where(mine, part, 0.0)
+        folded = part[0:rank, :]
+        for r in range(1, requests):
+            folded = folded + part[r * rank : (r + 1) * rank, :]
+        db[h] = folded
+        return mine, exchange(db, ds_, dr)
+
+    stages = [stage_a, stage_b, stage_c, stage_d, stage_t, stage_e]
+    for step in range(per + len(stages) - 1):
+        for i, stage in enumerate(stages):
+            if 0 <= step - i < per:
+                stage(step - i)
+            if i == 3 and step - i == per - 1:
+                m_back.wait_recv()
+                mine, copies = adapter_down()
+        maps_at(step)
     for c in copies:
         c.wait()
     down = db[0]
@@ -355,10 +368,10 @@
     down = jnp.concatenate([down] * requests, axis=0)
     expand = jnp.where(mine, down, 0.0).astype(jnp.bfloat16)
     lift = lax.dot_general(
-        expand, maps_ref[wide : 2 * wide, :], (((0,), (0,)), ((), ())), preferred_element_type=jnp.float32
+        expand, tm[1], (((0,), (0,)), ((), ())), preferred_element_type=jnp.float32
     )
-    total = tot[...] + lift
-    tot[...] = total
+    total = acc_ref[...] + res_ref[...].astype(jnp.float32) + lift
+    acc_ref[...] = total
     mean = jnp.sum(total, axis=1, keepdims=True) / local
     off = total - mean
     square = jnp.sum(off * off, axis=1, keepdims=True)
@@ -378,54 +391,77 @@
     row = lax.broadcasted_iota(jnp.int32, (128, rows), 0)
     back = jnp.transpose(jnp.where(row == 0, mean, inv))
     normed_ref[...] = (
-        (tot[...] - back[:, 0:1]) * back[:, 1:2] * (1.0 + scale_ref[...]) + shift_ref[...]
+        (acc_ref[...] - back[:, 0:1]) * back[:, 1:2] * (1.0 + scale_ref[...]) + shift_ref[...]
     ).astype(jnp.bfloat16)
-
-
-def finish(acc, att, residual, maps, scale, shift, lengths, rank):
-    n_hid = lax.axis_size("hid")
-    rows, local = acc.shape
+    for cond, c in sends:
+        run(cond, lambda c=c: c.wait_send())
+
+
+def block(q, k, v, w, residual, bank_a, bank_b, scale, shift, lengths, adapters, slots):
+    n_tok, n_hid = lax.axis_size("tok"), lax.axis_size("hid")
+    rows, local = q.shape
+    rank = bank_a.shape[1]
+    requests = lengths.shape[0]
+    per = (local // HEAD_DIM + 1) // 2
     dma = pltpu.SemaphoreType.DMA
+    hbm = pl.BlockSpec(memory_space=pltpu.HBM)
     vm = pl.BlockSpec(memory_space=pltpu.VMEM)
+    sm = pl.BlockSpec(memory_space=pltpu.SMEM)
+    bf = jnp.bfloat16
+    maps = pltpu.VMEM((requests * rank, local), bf)
+    pair = pltpu.VMEM((2, requests * rank, local), bf)
     return pl.pallas_call(
-        functools.partial(finish_kernel, n_hid, lengths.shape[0], rank),
-        out_shape=(jax.ShapeDtypeStruct((rows, local), jnp.bfloat16),) * 2,
-        in_specs=[vm] * 6 + [pl.BlockSpec(memory_space=pltpu.SMEM)],
+        functools.partial(block_kernel, n_tok, n_hid, requests, rank),
+        out_shape=(jax.ShapeDtypeStruct((rows, local), bf),) * 2,
+        in_specs=[hbm] * 4 + [vm] * 5 + [sm] * 3,
         out_specs=(vm, vm),
         scratch_shapes=[
+            pltpu.VMEM((per, 2 * rows, HEAD_DIM), bf),
+            pltpu.VMEM((per, 2, 8 * rows, HEAD_DIM), bf),
+            pltpu.VMEM((per, rows, 2 * n_hid * HEAD_DIM), bf),
+            pltpu.VMEM((per, 2 * n_hid * HEAD_DIM, local), bf),
+            pltpu.VMEM((per, rows, HEAD_DIM), bf),
             pltpu.VMEM((rows, local), jnp.float32),
+            pltpu.VMEM((rows, local), bf),
+            pair, maps, maps, maps, maps, maps, pair,
             pltpu.VMEM((n_hid, rank, rows), jnp.float32),
             pltpu.VMEM((n_hid, 8, rows), jnp.float32),
+            dma((per, 2 * n_hid)),
+            dma((per, 3)),
+            dma((per, 3)),
+            dma((per, 3)),
+            dma((per, 2, 2)),
+            dma((per, 2, 2)),
+            dma((per, 2)),
+            dma((per, 2)),
+            dma((per, 2)),
+            dma((per, 2)),
+            dma((per,)),
+            dma((per,)),
+            dma((per, n_hid)),
+            dma((per, n_hid)),
+            dma((4,)),
+            dma((4,)),
             dma((n_hid - 1,)),
             dma((n_hid - 1,)),
             dma((n_hid - 1,)),
             dma((n_hid - 1,)),
         ],
         compiler_params=pltpu.CompilerParams(
-            collective_id=1, has_side_effects=True, vmem_limit_bytes=32 * 1024 * 1024
+            collective_id=0, has_side_effects=True, vmem_limit_bytes=48 * 1024 * 1024
         ),
-        name="adapter_norm",
-    )(acc, att, residual, maps, scale, shift, lengths)
+        name="block",
+    )(q, k, v, w, residual, bank_a, bank_b, scale, shift, lengths, adapters, slots)
 
 
 def on_device(
     queries, keys, values, residual, out_weight, adapter_a, adapter_b,
     request_lengths, request_adapter, adapter_slot, mod_scale, mod_shift,
 ):
-    held, local, rank = adapter_a.shape
-    requests = request_lengths.shape[0]
-    slots = adapter_slot[request_adapter] - lax.axis_index("tok") * held
-    here = ((slots >= 0) & (slots < held))[:, None, None]
-    slots = jnp.clip(slots, 0, held - 1)
-    take = lambda bank: jnp.stack(
-        [lax.dynamic_index_in_dim(bank, slots[r], 0, keepdims=False) for r in range(requests)]
+    return block(
+        queries, keys, values, out_weight, residual, jnp.transpose(adapter_a, (0, 2, 1)), adapter_b,
+        mod_scale[None, :], mod_shift[None, :], request_lengths, request_adapter, adapter_slot,
     )
-    a = jnp.where(here, jnp.transpose(take(adapter_a), (0, 2, 1)), 0)
-    b = jnp.where(here, take(adapter_b), 0)
-    maps = jnp.concatenate([a.reshape(requests * rank, local), b.reshape(requests * rank, local)], axis=0)
-    maps = lax.psum(maps, "tok")
-    acc, att = attention(queries, keys, values, out_weight, request_lengths)
-    return finish(acc, att, residual, maps, mod_scale[None, :], mod_shift[None, :], request_lengths, rank)
 
 
 def solution(mesh):

time: 119 us -> 94.6 us (0.79)
  between operations: 21.6 us -> 0.65 us
  other arithmetic: 1.68 us -> 0 us
  Pallas kernels: 83.6 us -> 82.2 us
    unnamed x18 -> x20, local copies, waits for them, and re-layouts: 6.58 us -> 9.93 us
    dynamic_slice x2 -> x0, local copies, waits for them, and re-layouts: 1.91 us -> none  [on_device(): lax.dynamic_index_in_dim(bank, slots[r], 0, keepdims=False)]
    pallas_call x2 -> x1, Pallas kernels: 83.6 us -> 82.2 us  [block(): pl.pallas_call(functools.partial(block_kernel, n_tok, n_hid, requests, ra...]
  transfers between devices with their start and end apart: 1 -> 0, of which waited for: 0 -> 0; matrix products, arithmetic and copies ran while one was open for 1% -> 0% of each run, Pallas kernels for 62% -> 0%
where the time goes in v2:
time: 94.6 us; the launch traced here: 94.1 us
  Pallas kernels  82.2 us (87%)
  local copies, waits for them, and re-layouts  11.3 us (12%)
    pallas_call x1, Pallas kernels, block(): pl.pallas_call(functools.partial(block_kernel, n_tok, n_hid, requests, ra...  82.2 us
    unnamed x20, local copies, waits for them, and re-layouts  9.93 us

profile of v2, /device:TPU:0, one launch (start us, length us, event | category | flops | bytes accessed | tf_op | source)
XLA Modules:
  0.0 94.1 jit_solution(12881008427498811850)
XLA Ops:
  0.6 0.7 broadcast_in_dim.6.scale_ref
  1.3 0.7 broadcast_in_dim.7.shift_ref
  2.0 0.0 copy-start
  2.0 1.1 %copy-done = bf16[256,1280]{1,0:T(8,128)(2,1)S(1)} copy-done((bf16[256,1280]{1,0:T(8,128)(2,1)S(1)}, bf16[256,1280]{1,0:T(8,128)(2,1)}, u32[]{:S(2)}) %copy-start) | copy-done | bytes 655384
  3.1 0.0 copy-start.1
  3.1 1.1 %copy-done.1 = bf16[256,1280]{1,0:T(8,128)(2,1)S(1)} copy-done((bf16[256,1280]{1,0:T(8,128)(2,1)S(1)}, bf16[256,1280]{1,0:T(8,128)(2,1)}, u32[]{:S(2)}) %copy-start.1) | copy-done | bytes 655384
  4.2 0.0 copy-start.2
  4.2 1.1 %copy-done.2 = bf16[256,1280]{1,0:T(8,128)(2,1)S(1)} copy-done((bf16[256,1280]{1,0:T(8,128)(2,1)S(1)}, bf16[256,1280]{1,0:T(8,128)(2,1)}, u32[]{:S(2)}) %copy-start.2) | copy-done | bytes 655384
  5.3 0.0 copy-start.3
  5.3 1.1 %copy-done.3 = bf16[256,1280]{1,0:T(8,128)(2,1)S(1)} copy-done((bf16[256,1280]{1,0:T(8,128)(2,1)S(1)}, bf16[256,1280]{1,0:T(8,128)(2,1)}, u32[]{:S(2)}) %copy-start.3) | copy-done | bytes 655384
  6.4 0.0 copy-start.4
  6.4 1.0 %copy-done.4 = bf16[8,1280,16]{1,2,0:T(8,128)(2,1)S(1)} copy-done((bf16[8,1280,16]{1,2,0:T(8,128)(2,1)S(1)}, bf16[8,1280,16]{1,2,0:T(8,128)(2,1)}, u32[]{:S(2)}) %copy-start.4) | copy-done | bytes 327704
  7.4 0.0 copy-start.5
  7.4 1.0 %copy-done.5 = bf16[8,16,1280]{2,1,0:T(8,128)(2,1)S(1)} copy-done((bf16[8,16,1280]{2,1,0:T(8,128)(2,1)S(1)}, bf16[8,16,1280]{2,1,0:T(8,128)(2,1)}, u32[]{:S(2)}) %copy-start.5) | copy-done | bytes 327704
  8.3 0.0 copy-start.6
  8.3 0.7 copy-done.6
  9.0 0.0 copy-start.7
  9.0 0.7 copy-done.7
  9.6 0.0 copy-start.8
  9.6 0.7 copy-done.8
  10.3 82.2 %block.1 = (bf16[256,1280]{1,0:T(8,128)(2,1)S(1)}, bf16[256,1280]{1,0:T(8,128)(2,1)S(1)}) custom-call(bf16[256,1280]{1,0:T(8,128)(2,1)S(1)} %copy-done, bf16[256,1280]{1,0:T(8,128)(2,1)S(1)} %copy-done.1, bf16[256,1280]{1,0:T(8,128)(2,1)S(1)} %copy-done.2, bf16[5120,1280]{1,0:T(8,128)(2,1)} %w_ref.1, bf16[256,1280]{1,0:T(8,128)(2,1)S(1)} %copy-done.3, ...), custom_call_target="tpu_custom_call" | custom-call | tf_op jit(solution)/shard_map/block/pallas_call | solution.py:413
  92.5 0.8 copy.16
  93.3 0.8 copy.17
Async XLA Ops:
  2.0 1.1 %copy-start = (bf16[256,1280]{1,0:T(8,128)(2,1)S(1)}, bf16[256,1280]{1,0:T(8,128)(2,1)}, u32[]{:S(2)}) copy-start(bf16[256,1280]{1,0:T(8,128)(2,1)} %q_ref.1) | copy-start | bytes 1966084
  3.1 1.1 %copy-start.1 = (bf16[256,1280]{1,0:T(8,128)(2,1)S(1)}, bf16[256,1280]{1,0:T(8,128)(2,1)}, u32[]{:S(2)}) copy-start(bf16[256,1280]{1,0:T(8,128)(2,1)} %k_ref.1) | copy-start | bytes 1966084
  4.2 1.1 %copy-start.2 = (bf16[256,1280]{1,0:T(8,128)(2,1)S(1)}, bf16[256,1280]{1,0:T(8,128)(2,1)}, u32[]{:S(2)}) copy-start(bf16[256,1280]{1,0:T(8,128)(2,1)} %v_ref.1) | copy-start | bytes 1966084
  5.3 1.1 %copy-start.3 = (bf16[256,1280]{1,0:T(8,128)(2,1)S(1)}, bf16[256,1280]{1,0:T(8,128)(2,1)}, u32[]{:S(2)}) copy-start(bf16[256,1280]{1,0:T(8,128)(2,1)} %res_ref.1) | copy-start | bytes 1966084
  6.4 1.0 %copy-start.4 = (bf16[8,1280,16]{1,2,0:T(8,128)(2,1)S(1)}, bf16[8,1280,16]{1,2,0:T(8,128)(2,1)}, u32[]{:S(2)}) copy-start(bf16[8,1280,16]{1,2,0:T(8,128)(2,1)} %param.17) | copy-start | bytes 983044
  7.4 1.0 %copy-start.5 = (bf16[8,16,1280]{2,1,0:T(8,128)(2,1)S(1)}, bf16[8,16,1280]{2,1,0:T(8,128)(2,1)}, u32[]{:S(2)}) copy-start(bf16[8,16,1280]{2,1,0:T(8,128)(2,1)} %b_ref.1) | copy-start | bytes 983044
  8.3 0.7 copy-start.6
  9.0 0.7 copy-start.7
  9.6 0.7 copy-start.8

commit v3 on v2

--- a/solution.py
+++ b/solution.py
@@ -52,7 +52,7 @@
     q_ref, k_ref, v_ref, w_ref, res_ref, a_ref, b_ref, scale_ref, shift_ref, len_ref, req_ref, slot_ref,
     stream_ref, normed_ref,
     qb, kv, ag, wb, ob, acc_ref, att_ref, mo, mi, cu, cd, fu, fd, tm, db, sb,
-    w_sem, l_sem, ys, yr, zs, zr, ps, pr, fs, fr, as_, ar, hs, hr, ms, mr, ds_, dr, ss_, sr,
+    w_sem, l_sem, ys, yr, zs, zr, ps, pr, fs, fr, as_, ar, hs, hr, ms, mr, ds_, dr, ss_, sr, i_sem, a_buf, b_buf, res_buf,
 ):
     rows, local = q_ref.shape
     hc = HEAD_DIM
@@ -89,14 +89,27 @@
 
     ways = [(has_up, up, base - 2 * rows, has_down), (has_down, down, base + 2 * rows, has_up)]
 
+    b_copies = [
+        pltpu.make_async_copy(src, dst, i_sem.at[i]) for i, (src, dst) in enumerate(((a_ref, a_buf), (b_ref, b_buf)))
+    ]
+    r_copy = pltpu.make_async_copy(res_ref, res_buf, i_sem.at[2])
+    for c in b_copies:
+        c.start()
+
     wide = requests * rank
     held = a_ref.shape[0]
-    for i, bank in enumerate((a_ref, b_ref)):
-        for r in range(requests):
-            slot = slot_ref[req_ref[r]] - tok * held
-            held_here = (slot >= 0) & (slot < held)
-            got = bank[jnp.clip(slot, 0, held - 1)]
-            mo[i, r * rank : (r + 1) * rank, :] = jnp.where(held_here, got, jnp.zeros_like(got))
+
+    def adapter_maps():
+        for c in b_copies:
+            c.wait()
+        for i, bank in enumerate((a_buf, b_buf)):
+            for r in range(requests):
+                slot = slot_ref[req_ref[r]] - tok * held
+                held_here = (slot >= 0) & (slot < held)
+                got = bank[jnp.clip(slot, 0, held - 1)]
+                mo[i, r * rank : (r + 1) * rank, :] = jnp.where(held_here, got, jnp.zeros_like(got))
+        m_pair.start()
+
     m_pair = remote(mo.at[1 - y], mi, ms.at[0], mr.at[0], partner)
     m_up = remote(fu, cu, ms.at[1], mr.at[1], up)
     m_down = remote(fd, cd, ms.at[2], mr.at[2], down)
@@ -138,8 +151,9 @@
 
     sends.extend([(None, m_pair), (has_up, m_up), (has_down, m_down), (None, m_back)])
 
-    y_copies, l_copies, z_copies = [], [], []
-    for j in range(per):
+    y_copies, l_copies, z_copies, w_copies = [], [], [], []
+
+    def stage_s(j):
         yc, lc, zc = [], [], []
         for i, (ref, at) in enumerate(((k_ref, kv), (v_ref, kv), (q_ref, qb))):
             src = ref.at[:, cols(oth_cols, j)]
@@ -162,9 +176,7 @@
         l_copies.append(lc)
         z_copies.append(zc)
 
-    m_pair.start()
-    w_copies = []
-    for j in range(per):
+    def stage_w(j):
         wc = []
         for g in range(2 * n_hid):
             row = (g // 2) * local + (g % 2) * second * hc + j * hc
@@ -177,6 +189,11 @@
             c.start()
             wc.append(c)
         w_copies.append(wc)
+
+    ahead = 2
+    for j in range(min(ahead, per)):
+        stage_s(j)
+    adapter_maps()
 
     @pl.when(p == 0)
     def _():
@@ -356,6 +373,12 @@
         for i, stage in enumerate(stages):
             if 0 <= step - i < per:
                 stage(step - i)
+            if i == 0 and step < per:
+                if step + ahead < per:
+                    stage_s(step + ahead)
+                stage_w(step)
+                if step == per - 1:
+                    r_copy.start()
             if i == 3 and step - i == per - 1:
                 m_back.wait_recv()
                 mine, copies = adapter_down()
@@ -370,7 +393,8 @@
     lift = lax.dot_general(
         expand, tm[1], (((0,), (0,)), ((), ())), preferred_element_type=jnp.float32
     )
-    total = acc_ref[...] + res_ref[...].astype(jnp.float32) + lift
+    r_copy.wait()
+    total = acc_ref[...] + res_buf[...].astype(jnp.float32) + lift
     acc_ref[...] = total
     mean = jnp.sum(total, axis=1, keepdims=True) / local
     off = total - mean
@@ -391,7 +415,7 @@
     row = lax.broadcasted_iota(jnp.int32, (128, rows), 0)
     back = jnp.transpose(jnp.where(row == 0, mean, inv))
     normed_ref[...] = (
-        (acc_ref[...] - back[:, 0:1]) * back[:, 1:2] * (1.0 + scale_ref[...]) + shift_ref[...]
+        (acc_ref[...] - back[:, 0:1]) * back[:, 1:2] * (1.0 + scale_ref[...].reshape(1, local)) + shift_ref[...].reshape(1, local)
     ).astype(jnp.bfloat16)
     for cond, c in sends:
         run(cond, lambda c=c: c.wait_send())
@@ -413,7 +437,7 @@
     return pl.pallas_call(
         functools.partial(block_kernel, n_tok, n_hid, requests, rank),
         out_shape=(jax.ShapeDtypeStruct((rows, local), bf),) * 2,
-        in_specs=[hbm] * 4 + [vm] * 5 + [sm] * 3,
+        in_specs=[hbm] * 7 + [vm] * 2 + [sm] * 3,
         out_specs=(vm, vm),
         scratch_shapes=[
             pltpu.VMEM((per, 2 * rows, HEAD_DIM), bf),
@@ -446,9 +470,13 @@
             dma((n_hid - 1,)),
             dma((n_hid - 1,)),
             dma((n_hid - 1,)),
+            dma((3,)),
+            pltpu.VMEM(bank_a.shape, bf),
+            pltpu.VMEM(bank_b.shape, bf),
+            pltpu.VMEM((rows, local), bf),
         ],
         compiler_params=pltpu.CompilerParams(
-            collective_id=0, has_side_effects=True, vmem_limit_bytes=48 * 1024 * 1024
+            collective_id=0, has_side_effects=True, vmem_limit_bytes=60 * 1024 * 1024
         ),
         name="block",
     )(q, k, v, w, residual, bank_a, bank_b, scale, shift, lengths, adapters, slots)
@@ -460,7 +488,7 @@
 ):
     return block(
         queries, keys, values, out_weight, residual, jnp.transpose(adapter_a, (0, 2, 1)), adapter_b,
-        mod_scale[None, :], mod_shift[None, :], request_lengths, request_adapter, adapter_slot,
+        mod_scale, mod_shift, request_lengths, request_adapter, adapter_slot,
     )
 
 

time: 94.6 us -> 81.7 us (0.86)
  local copies, waits for them, and re-layouts: 11.3 us -> 3.93 us
  Pallas kernels: 82.2 us -> 76.8 us
    unnamed x20 -> x2, local copies, waits for them, and re-layouts: 9.93 us -> 3.93 us
    pallas_call x1, Pallas kernels: 82.2 us -> 76.8 us  [block(): pl.pallas_call(functools.partial(block_kernel, n_tok, n_hid, requests, ra...]
    broadcast_in_dim x2 -> x0, local copies, waits for them, and re-layouts: 1.4 us -> none  [the longest x1 0.7 us: on_device(): mod_scale[None, :]]
where the time goes in v3:
time: 81.7 us; the launch traced here: 81.4 us
  Pallas kernels  76.8 us (94%)
  local copies, waits for them, and re-layouts  3.93 us (5%)
    pallas_call x1, Pallas kernels, block(): pl.pallas_call(functools.partial(block_kernel, n_tok, n_hid, requests, ra...  76.8 us
    unnamed x2, local copies, waits for them, and re-layouts  3.93 us

profile of v3, /device:TPU:0, one launch (start us, length us, event | category | flops | bytes accessed | tf_op | source)
XLA Modules:
  0.0 81.4 jit_solution(15547968589861740490)
XLA Ops:
  0.6 76.8 %block.1 = (bf16[256,1280]{1,0:T(8,128)(2,1)}, bf16[256,1280]{1,0:T(8,128)(2,1)}) custom-call(bf16[256,1280]{1,0:T(8,128)(2,1)} %q_ref.1, bf16[256,1280]{1,0:T(8,128)(2,1)} %k_ref.1, bf16[256,1280]{1,0:T(8,128)(2,1)} %v_ref.1, bf16[5120,1280]{1,0:T(8,128)(2,1)} %w_ref.1, bf16[256,1280]{1,0:T(8,128)(2,1)} %res_ref.1, bf16[8,16,1280]{2,1,0:T(8,128)(2,1)} %bitcast.1, ...), custom_call_target="tpu_custom_call" | custom-call | tf_op jit(solution)/shard_map/block/pallas_call | solution.py:437
  77.5 2.0 %copy.16 = bf16[256,1280]{1,0:T(8,128)(2,1)} copy(bf16[256,1280]{1,0:T(8,128)(2,1)} %get-tuple-element.4) | data formatting | bytes 1310720
  79.4 2.0 %copy.17 = bf16[256,1280]{1,0:T(8,128)(2,1)} copy(bf16[256,1280]{1,0:T(8,128)(2,1)} %get-tuple-element.5) | data formatting | bytes 1310720
